TPU v7x, 32 devices: a whole 2x2x4 slice. The times are simulated.
32 devices in a mesh: grp: 2 (over y), row: 4 (over z), col: 2 (over x), rep: 2 (over core).
Axes of the slice: x: 2, y: 2, z: 4, core: 2. Of those that a mesh axis runs over, the one named last changes fastest.
Arguments:
- features: bfloat16 [4096, 256], P(('grp', 'row', 'col', 'rep')), parts along dimension 0, may hold values from -6 to 6
- cotangent: bfloat16 [4096, 256], P(('grp', 'row', 'col', 'rep')), parts along dimension 0, may hold values from -6 to 6
- weight: bfloat16 [256, 256], replicated, may hold values from -0.375 to 0.375
- bias: float32 [256], replicated, may hold values from -3 to 3
- tile_values: bfloat16 [8, 4, 16, 128, 128], P(('grp', 'row'), ('col', 'rep')), parts along dimension 0, may hold values from -0.3125 to 0.3125
- tile_rows: int32 [8, 4, 16], P(('grp', 'row'), ('col', 'rep')), parts along dimension 0, may hold values from 0 to 3, as said below
- tile_cols: int32 [8, 4, 16], P(('grp', 'row'), ('col', 'rep')), parts along dimension 0, may hold values from 0 to 3
- tile_counts: int32 [8, 4], P(('grp', 'row'), ('col', 'rep')), parts along dimension 0, may hold values from 1 to 16, as said below
Outputs:
- activated: bfloat16 [4096, 256], P(('grp', 'row', 'col', 'rep')), parts along dimension 0
- grad_features: bfloat16 [4096, 256], P(('grp', 'row', 'col', 'rep')), parts along dimension 0
- grad_weight: float32 [512, 256], P('grp'), parts along dimension 0
There are 2 independent parts, one for each index of `grp`. A program takes and returns all parts, laid end to end along the dimension named above; an argument that names none is the same for every part. Nothing has to cross between parts.
Inputs may be any that keep to these rules, and one draw needn't show every extreme that they name: Within one block the pairs (tile_rows, tile_cols) of the listed tiles are distinct. Only the first tile_counts[r, b] listed tiles of a block are nonzero; the rest are ignored. Some block holds exactly 16 tiles in every draw.
All inputs are finite; a program needn't handle non-finite values.
Results may differ from a plain program's by a relative error of at most 0.015.
Values may be sent and summed in bfloat16 or wider, within the bound.
A program may use at most 128 MiB of HBM per device.

v0:
```python
import math

import jax
import jax.numpy as jnp
from jax import lax
from jax.sharding import PartitionSpec as P


def onehot_rows(ids, count, width):
    live = jnp.arange(ids.shape[0]) < count
    hit = (ids[:, None] == jnp.arange(width)[None, :]) & live[:, None]
    return hit.astype(jnp.float32)


def forward_block(values, rows, cols, count, section, tile_size, row_tiles):
    width = section.shape[1]
    picked = section.reshape(-1, tile_size, width)[cols]
    prod = jnp.einsum("tab,tbf->taf", values, picked, preferred_element_type=jnp.float32)
    table = onehot_rows(rows, count, row_tiles)
    summed = jnp.einsum("ti,taf->iaf", table, prod, precision=lax.Precision.HIGHEST)
    return summed.reshape(row_tiles * tile_size, width)


def transposed_block(values, rows, cols, count, grads, tile_size, col_tiles):
    width = grads.shape[1]
    picked = grads.reshape(-1, tile_size, width)[rows]
    prod = jnp.einsum("tab,taf->tbf", values, picked, preferred_element_type=jnp.float32)
    table = onehot_rows(cols, count, col_tiles)
    summed = jnp.einsum("tj,tbf->jbf", table, prod, precision=lax.Precision.HIGHEST)
    return summed.reshape(col_tiles * tile_size, width)


def on_device(features, cotangent, weight, bias, tile_values, tile_rows, tile_cols, tile_counts):
    values = tile_values[0, 0]
    rows = tile_rows[0, 0]
    cols = tile_cols[0, 0]
    count = tile_counts[0, 0]
    tile_size = values.shape[1]
    pieces = features.shape[0]
    blocks_across = lax.axis_size(("col", "rep"))
    row_devices = lax.axis_size("row")
    row_tiles = blocks_across * pieces // tile_size
    col_tiles = row_devices * pieces // tile_size
    nodes = pieces * blocks_across * row_devices
    xw = jnp.dot(features, weight, preferred_element_type=jnp.float32).astype(jnp.bfloat16)
    section = lax.all_gather(xw, "row", axis=0, tiled=True)
    partial_value = forward_block(values, rows, cols, count, section, tile_size, row_tiles)
    total = lax.psum(partial_value.astype(jnp.bfloat16), ("col", "rep")).astype(jnp.float32)
    offset = lax.axis_index(("col", "rep")) * pieces
    own = lax.dynamic_slice_in_dim(total, offset, pieces, 0)
    pre = own + bias[None, :]
    activated = jax.nn.silu(pre).astype(jnp.bfloat16)
    sig = jax.nn.sigmoid(pre)
    grad_pre = (cotangent.astype(jnp.float32) * sig * (1.0 + pre * (1.0 - sig))).astype(
        jnp.bfloat16
    )
    row_grads = lax.all_gather(grad_pre, ("col", "rep"), axis=0, tiled=True)
    term = transposed_block(values, rows, cols, count, row_grads, tile_size, col_tiles)
    grad_xw = lax.psum_scatter(term.astype(jnp.bfloat16), "row", scatter_dimension=0, tiled=True)
    grad_features = lax.dot_general(
        grad_xw, weight, (((1,), (1,)), ((), ())), preferred_element_type=jnp.float32
    ).astype(jnp.bfloat16)
    local_grad = lax.dot_general(
        features, grad_xw, (((0,), (0,)), ((), ())), preferred_element_type=jnp.float32
    )
    grad_weight = lax.psum(local_grad, ("row", "col", "rep")) * (1.0 / math.sqrt(nodes))
    return (activated, grad_features, grad_weight)


def solution(mesh):
    placed = (
        P(("grp", "row", "col", "rep"), None),
        P(("grp", "row", "col", "rep"), None),
        P(),
        P(),
        P(("grp", "row"), ("col", "rep"), None, None, None),
        P(("grp", "row"), ("col", "rep"), None),
        P(("grp", "row"), ("col", "rep"), None),
        P(("grp", "row"), ("col", "rep")),
    )
    return jax.shard_map(
        on_device,
        mesh=mesh,
        in_specs=placed,
        out_specs=(
            P(("grp", "row", "col", "rep"), None),
            P(("grp", "row", "col", "rep"), None),
            P("grp", None),
        ),
        check_vma=False,
    )
```

profile of v0, /device:TPU:0, one launch (start us, length us, event | category | flops | bytes accessed | tf_op | source)
XLA Modules:
  0.0 202.6 jit_solution(7224361567972730764)
XLA Ops:
  7.2 0.0 copy-start
  7.2 0.0 all-reduce.3.cloned.1.call-start
  7.9 0.7 fusion.24
  8.6 1.1 convolution_convert_fusion.1
  9.7 15.6 %all_gather.6 = bf16[512,256]{1,0:T(8,128)(2,1)S(1)} all-gather(bf16[128,256]{1,0:T(8,128)(2,1)S(1)} %convolution_convert_fusion.1), channel_id=1, replica_groups=mesh['grp'=2,'row'=4,'col'=2,'rep'=2] {'row'}, dimensions={0}, use_global_device_ids=true | all-gather | bytes 327680 | tf_op jit(solution)/shard_map/all_gather | solution.py:46
  25.3 1.6 gather_fusion
  26.9 0.0 copy-done
  26.9 1.7 fusion.12
  28.6 0.0 copy-start.5
  28.6 2.1 %copy.15 = f32[16,256,128]{1,0,2:T(8,128)} copy(f32[16,256,128]{2,1,0:T(8,128)S(1)} %fusion.12) | data formatting | bytes 4194304 | tf_op jit(solution)/shard_map/tab,tbf->taf/dot_general | solution.py:18
  30.7 0.0 copy-start.3
  30.7 0.0 copy-start.4
  30.7 0.0 copy-done.5
  30.7 2.4 %fusion.4 = bf16[4,128,256]{2,0,1:T(4,128)(2,1)S(1)} fusion(f32[16,256,128]{1,0,2:T(8,128)} %copy.15, s32[16]{0:T(128)S(1)} %bitcast.51, pred[16]{0:T(512)(128)(4,1)S(1)} %iota_compare_fusion.2), kind=kOutput, calls=%fused_computation.6 | convolution fusion | flops 25297024 | bytes 2359376 | tf_op jit(solution)/shard_map/ti,taf->iaf/dot_general | solution.py:20
  33.2 0.7 copy.12
  33.9 0.0 all-reduce.3.cloned.1.call-update
  33.9 0.0 reduce-scatter.2.cloned.1.call-start
  34.0 33.6 %all-reduce.3.cloned.1.call-done = bf16[512,256]{1,0:T(8,128)(2,1)} async-done(((bf16[512,256]{1,0:T(8,128)(2,1)}), bf16[512,256]{1,0:T(8,128)(2,1)}) %all-reduce.3.cloned.1.call-update) | async-done | bytes 262160 | tf_op jit(solution)/shard_map/psum | solution.py:48
  67.6 0.0 copy-done.3
  67.6 0.0 copy-done.4
  67.6 1.5 multiply_convert_fusion
  69.1 5.8 %all_gather.7 = bf16[512,256]{1,0:T(8,128)(2,1)S(1)} all-gather(bf16[128,256]{1,0:T(8,128)(2,1)S(1)} %get-tuple-element.9), channel_id=1, replica_groups=mesh['grp'=2,'row'=4,'col'=2,'rep'=2] {'col','rep'}, dimensions={0}, use_global_device_ids=true | all-gather | bytes 327680 | tf_op jit(solution)/shard_map/all_gather | solution.py:57
  74.9 1.6 gather_fusion.1
  76.5 1.7 fusion.10
  78.2 0.0 copy-start.6
  78.2 2.1 %copy.16 = f32[16,256,128]{1,0,2:T(8,128)} copy(f32[16,256,128]{2,1,0:T(8,128)S(1)} %fusion.10) | data formatting | bytes 4194304 | tf_op jit(solution)/shard_map/tab,taf->tbf/dot_general | solution.py:27
  80.3 0.0 copy-start.2
  80.3 0.0 copy-start.1
  80.3 0.0 copy-done.6
  80.3 2.4 %fusion.7 = bf16[4,128,256]{2,0,1:T(4,128)(2,1)S(1)} fusion(f32[16,256,128]{1,0,2:T(8,128)} %copy.16, s32[16]{0:T(128)S(1)} %bitcast.52, pred[16]{0:T(512)(128)(4,1)S(1)} %iota_compare_fusion.2), kind=kOutput, calls=%fused_computation.7 | convolution fusion | flops 25297024 | bytes 2359376 | tf_op jit(solution)/shard_map/tj,tbf->jbf/dot_general | solution.py:29
  82.7 0.7 copy.13
  83.5 0.0 reduce-scatter.2.cloned.1.call-update
  83.5 0.0 all-reduce.5.cloned.1.call-start
  83.5 19.8 %reduce-scatter.2.cloned.1.call-done = bf16[128,256]{1,0:T(8,128)(2,1)} async-done(((bf16[512,256]{1,0:T(8,128)(2,1)}), bf16[128,256]{1,0:T(8,128)(2,1)}) %reduce-scatter.2.cloned.1.call-update) | async-done | bytes 65552 | tf_op jit(solution)/shard_map/reduce_scatter | solution.py:59
  103.3 0.0 copy-done.2
  103.3 1.8 convolution_bitcast_fusion
  105.0 0.0 all-reduce.5.cloned.1.call-update
  105.1 0.0 copy-done.1
  105.1 1.7 convolution_convert_fusion
  106.8 87.5 %all-reduce.5.cloned.1.call-done = f32[256,256]{0,1:T(8,128)} async-done(((f32[256,256]{0,1:T(8,128)}), f32[256,256]{0,1:T(8,128)}) %all-reduce.5.cloned.1.call-update) | async-done | bytes 262160 | tf_op jit(solution)/shard_map/psum | solution.py:66
  194.3 1.0 broadcast_multiply_fusion
  195.2 0.8 copy.14
  (4 shorter events, 0.0 us)
Async XLA Ops:
  7.2 19.8 %copy-start = (bf16[1,1,16,128,128]{4,3,2,1,0:T(8,128)(2,1)S(1)}, bf16[1,1,16,128,128]{4,3,2,1,0:T(8,128)(2,1)}, u32[]{:S(2)}) copy-start(bf16[1,1,16,128,128]{4,3,2,1,0:T(8,128)(2,1)} %param.12) | copy-start | bytes 1572868
  7.2 60.4 %all-reduce.3.cloned.1.call-start = ((), (), s32[]{:S(2)}) async-start(), calls=%async_computation.1 | async-start | bytes 524288 | tf_op jit(solution)/shard_map/psum | solution.py:48
  28.6 2.1 %copy-start.5 = (s32[1,1,16]{2,1,0:T(1,128)S(1)}, s32[1,1,16]{2,1,0:T(1,128)}, u32[]{:S(2)}) copy-start(s32[1,1,16]{2,1,0:T(1,128)} %param.13) | copy-start | bytes 196
  30.7 36.9 %copy-start.3 = (bf16[128,256]{1,0:T(8,128)(2,1)S(1)}, bf16[128,256]{1,0:T(8,128)(2,1)}, u32[]{:S(2)}) copy-start(bf16[128,256]{1,0:T(8,128)(2,1)} %param.9) | copy-start | bytes 196612
  30.7 36.9 %copy-start.4 = (f32[256]{0:T(256)S(1)}, f32[256]{0:T(256)}, u32[]{:S(2)}) copy-start(f32[256]{0:T(256)} %param.11) | copy-start | bytes 3076
  33.9 69.4 %reduce-scatter.2.cloned.1.call-start = ((), (), s32[]{:S(2)}) async-start(), calls=%async_computation.2 | async-start | bytes 327680 | tf_op jit(solution)/shard_map/reduce_scatter | solution.py:59
  78.2 2.1 %copy-start.6 = (s32[1,1,16]{2,1,0:T(1,128)S(1)}, s32[1,1,16]{2,1,0:T(1,128)}, u32[]{:S(2)}) copy-start(s32[1,1,16]{2,1,0:T(1,128)} %param.14) | copy-start | bytes 196
  80.3 23.0 %copy-start.2 = (bf16[128,256]{1,0:T(8,128)(2,1)S(1)}, bf16[128,256]{1,0:T(8,128)(2,1)}, u32[]{:S(2)}) copy-start(bf16[128,256]{1,0:T(8,128)(2,1)} %param.8) | copy-start | bytes 196612
  80.3 24.8 %copy-start.1 = (bf16[256,256]{1,0:T(8,128)(2,1)S(1)}, bf16[256,256]{1,0:T(8,128)(2,1)}, u32[]{:S(2)}) copy-start(bf16[256,256]{1,0:T(8,128)(2,1)} %param.10) | copy-start | bytes 393220
  83.5 110.8 %all-reduce.5.cloned.1.call-start = ((), (), s32[]{:S(2)}) async-start(), calls=%async_computation.3 | async-start | bytes 524288 | tf_op jit(solution)/shard_map/psum | solution.py:66
Sparse Core Ops, SparseCore 0:
  34.0 33.5 all-reduce.2
  83.6 19.6 reduce-scatter.1
  107.3 86.9 all-reduce.4
where the time goes:
time: 203 us
  waiting for transfers between devices  141 us (69%)
  blocking collectives  21.4 us (11%)
  between operations  14.5 us (7%)
  matrix products  12.8 us (6%)
  local copies, waits for them, and re-layouts  9.64 us (5%)
  other arithmetic  3.19 us (2%)
    psum x1, waiting for transfers between devices, on_device(): lax.psum(local_grad, ('row', 'col', 'rep')) * (1.0 / math.sqrt(nodes))  87.5 us
    psum x1, waiting for transfers between devices, on_device(): lax.psum(partial_value.astype(jnp.bfloat16), ('col', 'rep'))  33.6 us
    reduce_scatter x1, waiting for transfers between devices, on_device(): lax.psum_scatter(term.astype(jnp.bfloat16), 'row', scatter_dimension=0, t...  19.8 us
    all_gather x1, blocking collectives, on_device(): section = lax.all_gather(xw, 'row', axis=0, tiled=True)  15.6 us
    all_gather x1, blocking collectives, on_device(): row_grads = lax.all_gather(grad_pre, ('col', 'rep'), axis=0, tiled=True)  5.77 us
  transfers between devices with their start and end apart: 3, of which 3 were waited for; matrix products, arithmetic and copies ran while one was open for 1% of the time, Pallas kernels for 0%

commit v1 on v0

v1 whole, which is shorter than its diff:
```python
import functools
import math

import jax
import jax.numpy as jnp
from jax import lax
from jax.experimental import pallas as pl
from jax.experimental.pallas import tpu as pltpu
from jax.sharding import PartitionSpec as P

HALVES = 2
BF = jnp.bfloat16
F32 = jnp.float32


def kernel(
    sizes,
    rows_ref,
    cols_ref,
    count_ref,
    feat_hbm,
    cot_hbm,
    weight_hbm,
    bias_hbm,
    vals_hbm,
    act_ref,
    gf_ref,
    gw_ref,
    vals,
    dense,
    dense_t,
    weight,
    bias,
    cot,
    feats,
    part,
    part_in,
    own_h,
    all_h,
    term,
    term_in,
    gw_own,
    gw_in,
    gw_sum,
    gw_slice_in,
    gw_slices,
    gw_all,
    local_sem,
    feat_send,
    feat_recv,
    part_send,
    part_recv,
    h_send,
    h_recv,
    term_send,
    term_recv,
    gw1_send,
    gw1_recv,
    gw2_send,
    gw2_recv,
    gw3_send,
    gw3_recv,
    gw4_send,
    gw4_recv,
):
    n_row, n_col, n_rep, n_tiles, row_tiles, col_tiles, tile, wide, scale = sizes
    n_blk = n_col * n_rep
    half = wide // HALVES
    me_r = lax.axis_index("row")
    me_c = lax.axis_index("col")
    me_p = lax.axis_index("rep")
    me_b = me_c * n_rep + me_p

    def row_to(k):
        return lax.rem(me_r + k, n_row)

    def blk_to(k):
        return lax.rem(me_b + k, n_blk)

    def row_dev(r):
        return {"row": r}

    def blk_dev(b):
        return {"col": b // n_rep, "rep": lax.rem(b, n_rep)}

    def remote(src, dst, send, recv, dev):
        return pltpu.make_async_remote_copy(
            src_ref=src,
            dst_ref=dst,
            send_sem=send,
            recv_sem=recv,
            device_id=dev,
            device_id_type=pl.DeviceIdType.MESH,
        )

    def cut(ref, h):
        return ref.at[:, pl.ds(h * half, half)]

    own_feats = [
        pltpu.make_async_copy(cut(feat_hbm, h), feats.at[h, me_r], local_sem.at[4 + h])
        for h in range(HALVES)
    ]
    load_vals = pltpu.make_async_copy(vals_hbm, vals, local_sem.at[0])
    load_weight = pltpu.make_async_copy(weight_hbm, weight, local_sem.at[1])
    load_bias = pltpu.make_async_copy(bias_hbm, bias, local_sem.at[2])
    load_cot = pltpu.make_async_copy(cot_hbm, cot, local_sem.at[3])
    for c in own_feats:
        c.start()
    load_vals.start()
    load_weight.start()
    load_bias.start()
    load_cot.start()

    barrier = pltpu.get_barrier_semaphore()
    for k in range(1, n_row):
        pl.semaphore_signal(
            barrier, inc=1, device_id=row_dev(row_to(k)), device_id_type=pl.DeviceIdType.MESH
        )
    for k in range(1, n_blk):
        pl.semaphore_signal(
            barrier, inc=1, device_id=blk_dev(blk_to(k)), device_id_type=pl.DeviceIdType.MESH
        )
    pl.semaphore_wait(barrier, n_row + n_blk - 2)

    sends = []
    for h in range(HALVES):
        for k in range(1, n_row):
            c = remote(
                cut(feat_hbm, h),
                feats.at[h, me_r],
                feat_send.at[h, k],
                feat_recv.at[h, me_r],
                row_dev(row_to(k)),
            )
            c.start()
            sends.append(c)

    load_vals.wait()
    count = count_ref[0]

    def code_of(t):
        return jnp.where(t < count, rows_ref[t] * col_tiles + cols_ref[t], -1)

    small = n_tiles * row_tiles * col_tiles <= 256
    codes = [code_of(t) for t in range(n_tiles)] if small else None

    def place(p, i, j):
        if small:
            idx = jnp.int32(-1)
            for t in range(n_tiles):
                idx = jnp.where(codes[t] == p, t, idx)
        else:
            idx = lax.fori_loop(
                0,
                n_tiles,
                lambda t, cur: jnp.where(code_of(t) == p, t, cur),
                jnp.int32(-1),
            )
        got = vals[jnp.maximum(idx, 0)]
        got = jnp.where(idx >= 0, got, jnp.zeros_like(got))
        dense[pl.ds(i * tile, tile), pl.ds(j * tile, tile)] = got
        dense_t[pl.ds(j * tile, tile), pl.ds(i * tile, tile)] = got.T

    if small:
        for p in range(row_tiles * col_tiles):
            place(p, p // col_tiles, p % col_tiles)
    else:

        def step(p, carry):
            i = p // col_tiles
            place(p, pl.multiple_of(i, 1), p - i * col_tiles)
            return carry

        lax.fori_loop(0, row_tiles * col_tiles, step, 0)

    for h in range(HALVES):
        own_feats[h].wait()
        for k in range(1, n_row):
            src = row_to(k)
            remote(
                feats.at[h, src], feats.at[h, src], feat_send.at[h, k], feat_recv.at[h, src], row_dev(src)
            ).wait_recv()
        section = feats[h].reshape(n_row * tile, half)
        part[h] = jnp.dot(dense[...], section, preferred_element_type=F32).astype(BF)
        for k in range(n_blk - 1, 0, -1):
            b = blk_to(k)
            c = remote(
                part.at[h, pl.ds(pl.multiple_of(b * tile, tile), tile)],
                part_in.at[h, k],
                part_send.at[h, k],
                part_recv.at[h, k],
                blk_dev(b),
            )
            c.start()
            sends.append(c)

    load_weight.wait()
    load_bias.wait()
    load_cot.wait()
    pre = jnp.broadcast_to(bias[...], (tile, wide))
    agg = []
    for h in range(HALVES):
        total = part[h, pl.ds(pl.multiple_of(me_b * tile, tile), tile)].astype(F32)
        for k in range(1, n_blk):
            remote(
                part_in.at[h, k], part_in.at[h, k], part_send.at[h, k], part_recv.at[h, k], blk_dev(blk_to(k))
            ).wait_recv()
            total = total + part_in[h, k].astype(F32)
        total = total.astype(BF)
        agg.append(total)
        pre = pre + jnp.dot(total, weight[pl.ds(h * half, half), :], preferred_element_type=F32)

    sig = jax.nn.sigmoid(pre)
    grad = (cot[...].astype(F32) * sig * (1.0 + pre * (1.0 - sig))).astype(BF)
    for h in range(HALVES):
        piece = lax.dot_general(
            grad,
            weight[pl.ds(h * half, half), :],
            (((1,), (1,)), ((), ())),
            preferred_element_type=F32,
        ).astype(BF)
        own_h[h] = piece
        all_h[h, me_b] = piece
        for k in range(n_blk - 1, 0, -1):
            c = remote(
                own_h.at[h],
                all_h.at[h, me_b],
                h_send.at[h, k],
                h_recv.at[h, me_b],
                blk_dev(blk_to(k)),
            )
            c.start()
            sends.append(c)

    act_ref[...] = (pre * sig).astype(BF)

    rows1 = wide // n_blk
    for h in range(HALVES):
        gw_own[pl.ds(h * half, half), :] = (
            lax.dot_general(agg[h], grad, (((0,), (0,)), ((), ())), preferred_element_type=F32) * scale
        ).astype(BF)
    for k in range(1, n_blk):
        b = blk_to(k)
        c = remote(
            gw_own.at[pl.ds(pl.multiple_of(b * rows1, rows1), rows1)],
            gw_in.at[k],
            gw1_send.at[k],
            gw1_recv.at[k],
            blk_dev(b),
        )
        c.start()
        sends.append(c)

    for h in range(HALVES):
        for k in range(1, n_blk):
            src = blk_to(k)
            remote(
                all_h.at[h, src], all_h.at[h, src], h_send.at[h, k], h_recv.at[h, src], blk_dev(src)
            ).wait_recv()
        term[h] = jnp.dot(
            dense_t[...], all_h[h].reshape(n_blk * tile, half), preferred_element_type=F32
        ).astype(BF)
        for k in range(1, n_row):
            r = row_to(k)
            c = remote(
                term.at[h, pl.ds(pl.multiple_of(r * tile, tile), tile)],
                term_in.at[h, k],
                term_send.at[h, k],
                term_recv.at[h, k],
                row_dev(r),
            )
            c.start()
            sends.append(c)

    total = gw_own[pl.ds(pl.multiple_of(me_b * rows1, rows1), rows1), :].astype(F32)
    for k in range(1, n_blk):
        remote(
            gw_in.at[k], gw_in.at[k], gw1_send.at[k], gw1_recv.at[k], blk_dev(blk_to(k))
        ).wait_recv()
        total = total + gw_in[k].astype(F32)
    gw_sum[...] = total.astype(BF)

    owners = min(n_row, rows1 // 16)
    rows2 = rows1 // owners

    def guarded(cond, fn):
        if owners == n_row:
            fn()
        else:
            pl.when(cond)(fn)

    def slice_copy(k):
        r = row_to(k)
        return remote(
            gw_sum.at[pl.ds(pl.multiple_of(lax.rem(r, owners) * rows2, rows2), rows2)],
            gw_slice_in.at[k],
            gw2_send.at[k],
            gw2_recv.at[k],
            row_dev(r),
        )

    def spread_copy(k):
        slot = lax.rem(me_r, owners)
        return remote(
            gw_slices.at[pl.ds(pl.multiple_of(slot * rows2, rows2), rows2)],
            gw_slices.at[pl.ds(pl.multiple_of(slot * rows2, rows2), rows2)],
            gw3_send.at[k],
            gw3_recv.at[slot],
            row_dev(row_to(k)),
        )

    for k in range(1, n_row):
        guarded(row_to(k) < owners, slice_copy(k).start)

    def finish_slice():
        slot = pl.multiple_of(lax.rem(me_r, owners) * rows2, rows2)
        acc = gw_sum[pl.ds(slot, rows2), :].astype(F32)
        for k in range(1, n_row):
            slice_copy(k).wait_recv()
            acc = acc + gw_slice_in[k].astype(F32)
        gw_slices[pl.ds(slot, rows2), :] = acc.astype(BF)
        for k in range(1, n_row):
            spread_copy(k).start()

    guarded(me_r < owners, finish_slice)

    for k in range(1, n_row):
        src = row_to(k)
        slot = lax.rem(src, owners)

        def wait_slice(src=src, slot=slot, k=k):
            view = gw_slices.at[pl.ds(pl.multiple_of(slot * rows2, rows2), rows2)]
            remote(view, view, gw3_send.at[k], gw3_recv.at[slot], row_dev(src)).wait_recv()

        guarded(src < owners, wait_slice)

    for k in range(n_blk - 1, 0, -1):
        c = remote(
            gw_slices,
            gw_all.at[me_b],
            gw4_send.at[k],
            gw4_recv.at[me_b],
            blk_dev(blk_to(k)),
        )
        c.start()
        sends.append(c)
    gw_all[me_b] = gw_slices[...]

    for h in range(HALVES):
        total = term[h, pl.ds(pl.multiple_of(me_r * tile, tile), tile)].astype(F32)
        for k in range(1, n_row):
            remote(
                term_in.at[h, k], term_in.at[h, k], term_send.at[h, k], term_recv.at[h, k], row_dev(row_to(k))
            ).wait_recv()
            total = total + term_in[h, k].astype(F32)
        gf_ref[:, pl.ds(h * half, half)] = total.astype(BF)

    for k in range(1, n_blk):
        src = blk_to(k)
        remote(
            gw_all.at[src], gw_all.at[src], gw4_send.at[k], gw4_recv.at[src], blk_dev(src)
        ).wait_recv()
    gw_ref[...] = gw_all[...].reshape(wide, wide).astype(F32)

    for c in sends:
        c.wait_send()
    for k in range(1, n_row):
        guarded(row_to(k) < owners, slice_copy(k).wait_send)
    for k in range(1, n_row):
        guarded(me_r < owners, spread_copy(k).wait_send)


def on_device(features, cotangent, weight, bias, tile_values, tile_rows, tile_cols, tile_counts):
    values = tile_values[0, 0]
    n_tiles, tile = values.shape[:2]
    pieces, wide = features.shape
    n_row, n_col, n_rep = (lax.axis_size(a) for a in ("row", "col", "rep"))
    n_blk = n_col * n_rep
    row_tiles = n_blk * pieces // tile
    col_tiles = n_row * pieces // tile
    half = wide // HALVES
    rows1 = wide // n_blk
    owners = min(n_row, rows1 // 16)
    rows2 = rows1 // owners
    scale = 1.0 / math.sqrt(pieces * n_blk * n_row)
    sizes = (n_row, n_col, n_rep, n_tiles, row_tiles, col_tiles, tile, wide, scale)
    vmem = pl.BlockSpec(memory_space=pltpu.VMEM)
    smem = pl.BlockSpec(memory_space=pltpu.SMEM)
    anyw = pl.BlockSpec(memory_space=pl.ANY)
    sem = pltpu.SemaphoreType.DMA
    return pl.pallas_call(
        functools.partial(kernel, sizes),
        out_shape=(
            jax.ShapeDtypeStruct((pieces, wide), BF),
            jax.ShapeDtypeStruct((pieces, wide), BF),
            jax.ShapeDtypeStruct((wide, wide), F32),
        ),
        in_specs=[smem, smem, smem, anyw, anyw, anyw, anyw, anyw],
        out_specs=(vmem, vmem, vmem),
        scratch_shapes=[
            pltpu.VMEM((n_tiles, tile, tile), BF),
            pltpu.VMEM((row_tiles * tile, col_tiles * tile), BF),
            pltpu.VMEM((col_tiles * tile, row_tiles * tile), BF),
            pltpu.VMEM((wide, wide), BF),
            pltpu.VMEM((1, wide), F32),
            pltpu.VMEM((pieces, wide), BF),
            pltpu.VMEM((HALVES, n_row, pieces, half), BF),
            pltpu.VMEM((HALVES, n_blk * pieces, half), BF),
            pltpu.VMEM((HALVES, n_blk, pieces, half), BF),
            pltpu.VMEM((HALVES, pieces, half), BF),
            pltpu.VMEM((HALVES, n_blk, pieces, half), BF),
            pltpu.VMEM((HALVES, n_row * pieces, half), BF),
            pltpu.VMEM((HALVES, n_row, pieces, half), BF),
            pltpu.VMEM((wide, wide), BF),
            pltpu.VMEM((n_blk, rows1, wide), BF),
            pltpu.VMEM((rows1, wide), BF),
            pltpu.VMEM((n_row, rows2, wide), BF),
            pltpu.VMEM((rows1, wide), BF),
            pltpu.VMEM((n_blk, rows1, wide), BF),
            sem((4 + HALVES,)),
            sem((HALVES, n_row)),
            sem((HALVES, n_row)),
            sem((HALVES, n_blk)),
            sem((HALVES, n_blk)),
            sem((HALVES, n_blk)),
            sem((HALVES, n_blk)),
            sem((HALVES, n_row)),
            sem((HALVES, n_row)),
            sem((n_blk,)),
            sem((n_blk,)),
            sem((n_row,)),
            sem((n_row,)),
            sem((n_row,)),
            sem((n_row,)),
            sem((n_blk,)),
            sem((n_blk,)),
        ],
        compiler_params=pltpu.CompilerParams(
            collective_id=0, has_side_effects=True, vmem_limit_bytes=60 * 1024 * 1024
        ),
    )(
        tile_rows.reshape(n_tiles),
        tile_cols.reshape(n_tiles),
        tile_counts.reshape(1),
        features,
        cotangent,
        weight,
        bias.reshape(1, wide),
        values,
    )


def solution(mesh):
    placed = (
        P(("grp", "row", "col", "rep"), None),
        P(("grp", "row", "col", "rep"), None),
        P(),
        P(),
        P(("grp", "row"), ("col", "rep"), None, None, None),
        P(("grp", "row"), ("col", "rep"), None),
        P(("grp", "row"), ("col", "rep"), None),
        P(("grp", "row"), ("col", "rep")),
    )
    return jax.shard_map(
        on_device,
        mesh=mesh,
        in_specs=placed,
        out_specs=(
            P(("grp", "row", "col", "rep"), None),
            P(("grp", "row", "col", "rep"), None),
            P("grp", None),
        ),
        check_vma=False,
    )
```

time: 203 us -> 43 us (0.21)
  waiting for transfers between devices: 141 us -> 0 us
  Pallas kernels: 0 us -> 37.8 us
  blocking collectives: 21.4 us -> 0 us
  between operations: 14.5 us -> 1.3 us
  matrix products: 12.8 us -> 0 us
  local copies, waits for them, and re-layouts: 9.64 us -> 3.69 us
  other arithmetic: 3.19 us -> 0 us
    psum x2 -> x0, waiting for transfers between devices: 121 us -> none  [the longest x1 87.5 us: on_device(): lax.psum(local_grad, ('row', 'col', 'rep')) * (1.0 / math.sqrt(nodes))]
    pallas_call x0 -> x1, Pallas kernels: none -> 37.8 us  [on_device(): pl.pallas_call(functools.partial(kernel, sizes), out_shape=(jax.ShapeDtyp...]
    all_gather x2 -> x0, blocking collectives: 21.4 us -> none  [the longest x1 15.6 us: on_device(): section = lax.all_gather(xw, 'row', axis=0, tiled=True)]
    reduce_scatter x1 -> x0, waiting for transfers between devices: 19.8 us -> none  [on_device(): lax.psum_scatter(term.astype(jnp.bfloat16), 'row', scatter_dimension=0, t...]
    dot_general x7 -> x0, matrix products: 12.8 us -> none  [the longest x1 2.44 us: transposed_block(): jnp.einsum('tj,tbf->jbf', table, prod, precision=lax.Precision.HIGHEST)]
    dot_general x2 -> x0, local copies, waits for them, and re-layouts: 4.14 us -> none  [the longest x1 2.07 us: forward_block(): jnp.einsum('tab,tbf->taf', values, picked, preferred_element_type=jnp.flo...]
    gather x2 -> x0, local copies, waits for them, and re-layouts: 3.16 us -> none  [the longest x1 1.58 us: forward_block(): picked = section.reshape(-1, tile_size, width)[cols]]
    unnamed x15 -> x5, local copies, waits for them, and re-layouts: 0.87 us -> 3.69 us
  transfers between devices with their start and end apart: 3 -> 0, of which waited for: 3 -> 0; matrix products, arithmetic and copies ran while one was open for 1% -> 0% of each run, Pallas kernels for 0% -> 0%
where the time goes in v1:
time: 43 us; the launch traced here: 42.8 us
  Pallas kernels  37.8 us (88%)
  local copies, waits for them, and re-layouts  3.69 us (9%)
  between operations  1.3 us (3%)
    pallas_call x1, Pallas kernels, on_device(): pl.pallas_call(functools.partial(kernel, sizes), out_shape=(jax.ShapeDtyp...  37.8 us
    unnamed x5, local copies, waits for them, and re-layouts  3.69 us

profile of v1, /device:TPU:0, one launch (start us, length us, event | category | flops | bytes accessed | tf_op | source)
XLA Modules:
  0.0 42.8 jit_solution(2640211900247821782)
XLA Ops:
  1.3 37.8 %shard_map.103 = (bf16[128,256]{1,0:T(8,128)(2,1)}, bf16[128,256]{1,0:T(8,128)(2,1)}, f32[256,256]{1,0:T(8,128)}) custom-call(s32[16]{0:T(128)} %bitcast.8, s32[16]{0:T(128)} %bitcast.9, s32[1]{0:T(128)} %bitcast.5.count_ref, bf16[128,256]{1,0:T(8,128)(2,1)} %feat_hbm.1, bf16[128,256]{1,0:T(8,128)(2,1)} %cot_hbm.1, bf16[256,256]{1,0:T(8,128)(2,1)} %weight_hbm.1, ...), custom_call_target="tpu_custom_call" | custom-call | tf_op jit(solution)/shard_map/pallas_call | solution.py:391
  39.1 0.0 copy-start
  39.1 1.5 %copy.15 = bf16[128,256]{1,0:T(8,128)(2,1)} copy(bf16[128,256]{1,0:T(8,128)(2,1)} %get-tuple-element.6) | data formatting | bytes 131072
  40.6 1.5 %copy.16 = bf16[128,256]{1,0:T(8,128)(2,1)} copy(bf16[128,256]{1,0:T(8,128)(2,1)} %get-tuple-element.7) | data formatting | bytes 131072
  42.1 0.0 copy-done
  42.1 0.7 %copy.17 = f32[256,256]{1,0:T(8,128)} copy(f32[256,256]{1,0:T(8,128)S(1)} %copy-done) | data formatting | bytes 524288
Async XLA Ops:
  39.1 3.0 %copy-start = (f32[256,256]{1,0:T(8,128)S(1)}, f32[256,256]{1,0:T(8,128)}, u32[]{:S(2)}) copy-start(f32[256,256]{1,0:T(8,128)} %get-tuple-element.8) | copy-start | bytes 786436

commit v2 on v1

--- a/solution.py
+++ b/solution.py
@@ -8,7 +8,7 @@
 from jax.experimental.pallas import tpu as pltpu
 from jax.sharding import PartitionSpec as P
 
-HALVES = 2
+HALVES = 1
 BF = jnp.bfloat16
 F32 = jnp.float32
 
@@ -35,23 +35,22 @@
     feats,
     part,
     part_in,
-    own_h,
-    all_h,
+    own_g,
+    all_g,
     term,
     term_in,
     gw_own,
     gw_in,
     gw_sum,
-    gw_slice_in,
-    gw_slices,
+    gw_blk,
     gw_all,
     local_sem,
     feat_send,
     feat_recv,
     part_send,
     part_recv,
-    h_send,
-    h_recv,
+    g_send,
+    g_recv,
     term_send,
     term_recv,
     gw1_send,
@@ -60,8 +59,6 @@
     gw2_recv,
     gw3_send,
     gw3_recv,
-    gw4_send,
-    gw4_recv,
 ):
     n_row, n_col, n_rep, n_tiles, row_tiles, col_tiles, tile, wide, scale = sizes
     n_blk = n_col * n_rep
@@ -75,7 +72,7 @@
         return lax.rem(me_r + k, n_row)
 
     def blk_to(k):
-        return lax.rem(me_b + k, n_blk)
+        return lax.rem(me_c + k // n_rep, n_col) * n_rep + lax.rem(me_p + k % n_rep, n_rep)
 
     def row_dev(r):
         return {"row": r}
@@ -213,52 +210,62 @@
     sig = jax.nn.sigmoid(pre)
     grad = (cot[...].astype(F32) * sig * (1.0 + pre * (1.0 - sig))).astype(BF)
     for h in range(HALVES):
-        piece = lax.dot_general(
-            grad,
-            weight[pl.ds(h * half, half), :],
-            (((1,), (1,)), ((), ())),
-            preferred_element_type=F32,
-        ).astype(BF)
-        own_h[h] = piece
-        all_h[h, me_b] = piece
+        piece = grad[:, h * half : (h + 1) * half]
+        own_g[h] = piece
+        all_g[h, me_b] = piece
         for k in range(n_blk - 1, 0, -1):
             c = remote(
-                own_h.at[h],
-                all_h.at[h, me_b],
-                h_send.at[h, k],
-                h_recv.at[h, me_b],
+                own_g.at[h],
+                all_g.at[h, me_b],
+                g_send.at[h, k],
+                g_recv.at[h, me_b],
                 blk_dev(blk_to(k)),
             )
             c.start()
             sends.append(c)
 
+    owners = min(n_row, wide // 16)
+    rows1 = wide // owners
+
+    def guarded(cond, fn):
+        if owners == n_row:
+            fn()
+        else:
+            pl.when(cond)(fn)
+
+    def chunk(r):
+        return pl.ds(pl.multiple_of(lax.rem(r, owners) * rows1, rows1), rows1)
+
+    for h in range(HALVES):
+        gw_own[pl.ds(h * half, half), :] = lax.dot_general(
+            agg[h], grad, (((0,), (0,)), ((), ())), preferred_element_type=F32
+        ).astype(BF)
+
+    def owner_copy(k):
+        r = row_to(k)
+        return remote(
+            gw_own.at[chunk(r)], gw_in.at[me_r], gw1_send.at[k], gw1_recv.at[me_r], row_dev(r)
+        )
+
+    def block_copy(k):
+        return remote(
+            gw_sum, gw_blk.at[me_b], gw2_send.at[k], gw2_recv.at[me_b], blk_dev(blk_to(k))
+        )
+
+    def final_copy(k):
+        view = gw_all.at[chunk(me_r)]
+        return remote(
+            view, view, gw3_send.at[k], gw3_recv.at[lax.rem(me_r, owners)], row_dev(row_to(k))
+        )
+
+    for k in range(1, n_row):
+        guarded(row_to(k) < owners, owner_copy(k).start)
+
     act_ref[...] = (pre * sig).astype(BF)
 
-    rows1 = wide // n_blk
-    for h in range(HALVES):
-        gw_own[pl.ds(h * half, half), :] = (
-            lax.dot_general(agg[h], grad, (((0,), (0,)), ((), ())), preferred_element_type=F32) * scale
-        ).astype(BF)
-    for k in range(1, n_blk):
-        b = blk_to(k)
-        c = remote(
-            gw_own.at[pl.ds(pl.multiple_of(b * rows1, rows1), rows1)],
-            gw_in.at[k],
-            gw1_send.at[k],
-            gw1_recv.at[k],
-            blk_dev(b),
-        )
-        c.start()
-        sends.append(c)
-
-    for h in range(HALVES):
-        for k in range(1, n_blk):
-            src = blk_to(k)
-            remote(
-                all_h.at[h, src], all_h.at[h, src], h_send.at[h, k], h_recv.at[h, src], blk_dev(src)
-            ).wait_recv()
+    def spread_term(h):
         term[h] = jnp.dot(
-            dense_t[...], all_h[h].reshape(n_blk * tile, half), preferred_element_type=F32
+            dense_t[...], all_g[h].reshape(n_blk * tile, half), preferred_element_type=F32
         ).astype(BF)
         for k in range(1, n_row):
             r = row_to(k)
@@ -272,102 +279,88 @@
             c.start()
             sends.append(c)
 
-    total = gw_own[pl.ds(pl.multiple_of(me_b * rows1, rows1), rows1), :].astype(F32)
-    for k in range(1, n_blk):
-        remote(
-            gw_in.at[k], gw_in.at[k], gw1_send.at[k], gw1_recv.at[k], blk_dev(blk_to(k))
-        ).wait_recv()
-        total = total + gw_in[k].astype(F32)
-    gw_sum[...] = total.astype(BF)
-
-    owners = min(n_row, rows1 // 16)
-    rows2 = rows1 // owners
-
-    def guarded(cond, fn):
-        if owners == n_row:
-            fn()
-        else:
-            pl.when(cond)(fn)
-
-    def slice_copy(k):
-        r = row_to(k)
-        return remote(
-            gw_sum.at[pl.ds(pl.multiple_of(lax.rem(r, owners) * rows2, rows2), rows2)],
-            gw_slice_in.at[k],
-            gw2_send.at[k],
-            gw2_recv.at[k],
-            row_dev(r),
-        )
-
-    def spread_copy(k):
-        slot = lax.rem(me_r, owners)
-        return remote(
-            gw_slices.at[pl.ds(pl.multiple_of(slot * rows2, rows2), rows2)],
-            gw_slices.at[pl.ds(pl.multiple_of(slot * rows2, rows2), rows2)],
-            gw3_send.at[k],
-            gw3_recv.at[slot],
-            row_dev(row_to(k)),
-        )
-
-    for k in range(1, n_row):
-        guarded(row_to(k) < owners, slice_copy(k).start)
-
-    def finish_slice():
-        slot = pl.multiple_of(lax.rem(me_r, owners) * rows2, rows2)
-        acc = gw_sum[pl.ds(slot, rows2), :].astype(F32)
-        for k in range(1, n_row):
-            slice_copy(k).wait_recv()
-            acc = acc + gw_slice_in[k].astype(F32)
-        gw_slices[pl.ds(slot, rows2), :] = acc.astype(BF)
-        for k in range(1, n_row):
-            spread_copy(k).start()
-
-    guarded(me_r < owners, finish_slice)
+    for h in range(HALVES):
+        for k in range(1, n_blk):
+            src = blk_to(k)
+            remote(
+                all_g.at[h, src], all_g.at[h, src], g_send.at[h, k], g_recv.at[h, src], blk_dev(src)
+            ).wait_recv()
+        if h < HALVES - 1:
+            spread_term(h)
+
+    spread_term(HALVES - 1)
+    def sum_rows():
+        gw_in[me_r] = gw_own[chunk(me_r), :]
+        for k in range(1, n_row):
+            src = row_to(k)
+            remote(
+                gw_in.at[src], gw_in.at[src], gw1_send.at[k], gw1_recv.at[src], row_dev(src)
+            ).wait_recv()
+        total = gw_in[0].astype(F32)
+        for r in range(1, n_row):
+            total = total + gw_in[r].astype(F32)
+        gw_sum[...] = total.astype(BF)
+        for k in range(n_blk - 1, 0, -1):
+            block_copy(k).start()
+
+    guarded(me_r < owners, sum_rows)
+
+    def total_chunk():
+        gw_blk[me_b] = gw_sum[...]
+        for k in range(1, n_blk):
+            src = blk_to(k)
+            remote(
+                gw_blk.at[src], gw_blk.at[src], gw2_send.at[k], gw2_recv.at[src], blk_dev(src)
+            ).wait_recv()
+        total = gw_blk[0].astype(F32)
+        for b in range(1, n_blk):
+            total = total + gw_blk[b].astype(F32)
+        gw_all[chunk(me_r), :] = total.astype(BF)
+        for k in range(1, n_row):
+            final_copy(k).start()
+
+    guarded(me_r < owners, total_chunk)
+
+    grad_feat = jnp.zeros((tile, wide), F32)
+    for h in range(HALVES):
+        total = term[h, pl.ds(pl.multiple_of(me_r * tile, tile), tile)].astype(F32)
+        for k in range(1, n_row):
+            remote(
+                term_in.at[h, k], term_in.at[h, k], term_send.at[h, k], term_recv.at[h, k], row_dev(row_to(k))
+            ).wait_recv()
+            total = total + term_in[h, k].astype(F32)
+        grad_feat = grad_feat + lax.dot_general(
+            total.astype(BF),
+            weight[:, pl.ds(h * half, half)],
+            (((1,), (1,)), ((), ())),
+            preferred_element_type=F32,
+        )
+    gf_ref[...] = grad_feat.astype(BF)
 
     for k in range(1, n_row):
         src = row_to(k)
-        slot = lax.rem(src, owners)
-
-        def wait_slice(src=src, slot=slot, k=k):
-            view = gw_slices.at[pl.ds(pl.multiple_of(slot * rows2, rows2), rows2)]
-            remote(view, view, gw3_send.at[k], gw3_recv.at[slot], row_dev(src)).wait_recv()
-
-        guarded(src < owners, wait_slice)
-
-    for k in range(n_blk - 1, 0, -1):
-        c = remote(
-            gw_slices,
-            gw_all.at[me_b],
-            gw4_send.at[k],
-            gw4_recv.at[me_b],
-            blk_dev(blk_to(k)),
-        )
-        c.start()
-        sends.append(c)
-    gw_all[me_b] = gw_slices[...]
-
-    for h in range(HALVES):
-        total = term[h, pl.ds(pl.multiple_of(me_r * tile, tile), tile)].astype(F32)
-        for k in range(1, n_row):
-            remote(
-                term_in.at[h, k], term_in.at[h, k], term_send.at[h, k], term_recv.at[h, k], row_dev(row_to(k))
-            ).wait_recv()
-            total = total + term_in[h, k].astype(F32)
-        gf_ref[:, pl.ds(h * half, half)] = total.astype(BF)
-
-    for k in range(1, n_blk):
-        src = blk_to(k)
-        remote(
-            gw_all.at[src], gw_all.at[src], gw4_send.at[k], gw4_recv.at[src], blk_dev(src)
-        ).wait_recv()
-    gw_ref[...] = gw_all[...].reshape(wide, wide).astype(F32)
+
+        def wait_chunk(src=src, k=k):
+            view = gw_all.at[chunk(src)]
+            remote(
+                view, view, gw3_send.at[k], gw3_recv.at[lax.rem(src, owners)], row_dev(src)
+            ).wait_recv()
+
+        guarded(src < owners, wait_chunk)
+    gw_ref[...] = gw_all[...].astype(F32) * scale
 
     for c in sends:
         c.wait_send()
     for k in range(1, n_row):
-        guarded(row_to(k) < owners, slice_copy(k).wait_send)
-    for k in range(1, n_row):
-        guarded(me_r < owners, spread_copy(k).wait_send)
+        guarded(row_to(k) < owners, owner_copy(k).wait_send)
+
+    def drain():
+        for k in range(1, n_blk):
+            block_copy(k).wait_send()
+        for k in range(1, n_row):
+            final_copy(k).wait_send()
+
+    guarded(me_r < owners, drain)
 
 
 def on_device(features, cotangent, weight, bias, tile_values, tile_rows, tile_cols, tile_counts):
@@ -379,21 +372,19 @@
     row_tiles = n_blk * pieces // tile
     col_tiles = n_row * pieces // tile
     half = wide // HALVES
-    rows1 = wide // n_blk
-    owners = min(n_row, rows1 // 16)
-    rows2 = rows1 // owners
+    rows1 = wide // min(n_row, wide // 16)
     scale = 1.0 / math.sqrt(pieces * n_blk * n_row)
     sizes = (n_row, n_col, n_rep, n_tiles, row_tiles, col_tiles, tile, wide, scale)
+    smem = pl.BlockSpec(memory_space=pltpu.SMEM)
     vmem = pl.BlockSpec(memory_space=pltpu.VMEM)
-    smem = pl.BlockSpec(memory_space=pltpu.SMEM)
     anyw = pl.BlockSpec(memory_space=pl.ANY)
     sem = pltpu.SemaphoreType.DMA
-    return pl.pallas_call(
+    outs = pl.pallas_call(
         functools.partial(kernel, sizes),
         out_shape=(
-            jax.ShapeDtypeStruct((pieces, wide), BF),
-            jax.ShapeDtypeStruct((pieces, wide), BF),
-            jax.ShapeDtypeStruct((wide, wide), F32),
+            pltpu.VMEM((pieces, wide), BF),
+            pltpu.VMEM((pieces, wide), BF),
+            pltpu.VMEM((wide, wide), F32),
         ),
         in_specs=[smem, smem, smem, anyw, anyw, anyw, anyw, anyw],
         out_specs=(vmem, vmem, vmem),
@@ -412,11 +403,10 @@
             pltpu.VMEM((HALVES, n_row * pieces, half), BF),
             pltpu.VMEM((HALVES, n_row, pieces, half), BF),
             pltpu.VMEM((wide, wide), BF),
-            pltpu.VMEM((n_blk, rows1, wide), BF),
-            pltpu.VMEM((rows1, wide), BF),
-            pltpu.VMEM((n_row, rows2, wide), BF),
+            pltpu.VMEM((n_row, rows1, wide), BF),
             pltpu.VMEM((rows1, wide), BF),
             pltpu.VMEM((n_blk, rows1, wide), BF),
+            pltpu.VMEM((wide, wide), BF),
             sem((4 + HALVES,)),
             sem((HALVES, n_row)),
             sem((HALVES, n_row)),
@@ -426,14 +416,12 @@
             sem((HALVES, n_blk)),
             sem((HALVES, n_row)),
             sem((HALVES, n_row)),
+            sem((n_row,)),
+            sem((n_row,)),
             sem((n_blk,)),
             sem((n_blk,)),
             sem((n_row,)),
             sem((n_row,)),
-            sem((n_row,)),
-            sem((n_row,)),
-            sem((n_blk,)),
-            sem((n_blk,)),
         ],
         compiler_params=pltpu.CompilerParams(
             collective_id=0, has_side_effects=True, vmem_limit_bytes=60 * 1024 * 1024
@@ -448,6 +436,7 @@
         bias.reshape(1, wide),
         values,
     )
+    return outs
 
 
 def solution(mesh):

time: 43 us -> 34.9 us (0.81)
  Pallas kernels: 37.8 us -> 31.4 us
  local copies, waits for them, and re-layouts: 3.69 us -> 1.96 us
    pallas_call x1, Pallas kernels: 37.8 us -> 31.4 us  [on_device(): pl.pallas_call(functools.partial(kernel, sizes), out_shape=(pltpu.VMEM((p...]
    unnamed x5 -> x3, local copies, waits for them, and re-layouts: 3.69 us -> 1.96 us
where the time goes in v2:
time: 34.9 us; the launch traced here: 34.7 us
  Pallas kernels  31.4 us (90%)
  local copies, waits for them, and re-layouts  1.96 us (6%)
  between operations  1.29 us (4%)
    pallas_call x1, Pallas kernels, on_device(): pl.pallas_call(functools.partial(kernel, sizes), out_shape=(pltpu.VMEM((p...  31.4 us
    unnamed x3, local copies, waits for them, and re-layouts  1.96 us

profile of v2, /device:TPU:0, one launch (start us, length us, event | category | flops | bytes accessed | tf_op | source)
XLA Modules:
  0.0 34.7 jit_solution(16345595188883118586)
XLA Ops:
  1.3 31.4 %shard_map.103 = (bf16[128,256]{1,0:T(8,128)(2,1)S(1)}, bf16[128,256]{1,0:T(8,128)(2,1)S(1)}, f32[256,256]{1,0:T(8,128)S(1)}) custom-call(s32[16]{0:T(128)} %bitcast.8, s32[16]{0:T(128)} %bitcast.9, s32[1]{0:T(128)} %bitcast.5.count_ref, bf16[128,256]{1,0:T(8,128)(2,1)} %feat_hbm.1, bf16[128,256]{1,0:T(8,128)(2,1)} %cot_hbm.1, bf16[256,256]{1,0:T(8,128)(2,1)} %weight_hbm.1, ...), custom_call_target="tpu_custom_call" | custom-call | tf_op jit(solution)/shard_map/pallas_call | solution.py:382
  32.7 0.6 %copy.14 = bf16[128,256]{1,0:T(8,128)(2,1)} copy(bf16[128,256]{1,0:T(8,128)(2,1)S(1)} %get-tuple-element.3) | data formatting | bytes 131072
  33.4 0.6 %copy.15 = bf16[128,256]{1,0:T(8,128)(2,1)} copy(bf16[128,256]{1,0:T(8,128)(2,1)S(1)} %get-tuple-element.4) | data formatting | bytes 131072
  34.0 0.7 %copy.16 = f32[256,256]{1,0:T(8,128)} copy(f32[256,256]{1,0:T(8,128)S(1)} %get-tuple-element.5) | data formatting | bytes 524288

commit v3 on v2

--- a/solution.py
+++ b/solution.py
@@ -59,6 +59,8 @@
     gw2_recv,
     gw3_send,
     gw3_recv,
+    gw4_send,
+    gw4_recv,
 ):
     n_row, n_col, n_rep, n_tiles, row_tiles, col_tiles, tile, wide, scale = sizes
     n_blk = n_col * n_rep
@@ -178,9 +180,12 @@
                 feats.at[h, src], feats.at[h, src], feat_send.at[h, k], feat_recv.at[h, src], row_dev(src)
             ).wait_recv()
         section = feats[h].reshape(n_row * tile, half)
-        part[h] = jnp.dot(dense[...], section, preferred_element_type=F32).astype(BF)
-        for k in range(n_blk - 1, 0, -1):
+        for k in range(n_blk - 1, -1, -1):
             b = blk_to(k)
+            mine = pl.ds(pl.multiple_of(b * tile, tile), tile)
+            part[h, mine] = jnp.dot(dense[mine, :], section, preferred_element_type=F32).astype(BF)
+            if k == 0:
+                break
             c = remote(
                 part.at[h, pl.ds(pl.multiple_of(b * tile, tile), tile)],
                 part_in.at[h, k],
@@ -241,6 +246,13 @@
             agg[h], grad, (((0,), (0,)), ((), ())), preferred_element_type=F32
         ).astype(BF)
 
+    def cols(p):
+        return pl.ds(pl.multiple_of(p * (wide // n_rep), wide // n_rep), wide // n_rep)
+
+    def core_copy(k):
+        view = gw_all.at[:, cols(me_p)]
+        return remote(view, view, gw4_send.at[k], gw4_recv.at[me_p], blk_dev(blk_to(k)))
+
     def owner_copy(k):
         r = row_to(k)
         return remote(
@@ -249,11 +261,15 @@
 
     def block_copy(k):
         return remote(
-            gw_sum, gw_blk.at[me_b], gw2_send.at[k], gw2_recv.at[me_b], blk_dev(blk_to(k))
+            gw_sum.at[:, cols(lax.rem(blk_to(k), n_rep))],
+            gw_blk.at[me_b],
+            gw2_send.at[k],
+            gw2_recv.at[me_b],
+            blk_dev(blk_to(k)),
         )
 
     def final_copy(k):
-        view = gw_all.at[chunk(me_r)]
+        view = gw_all.at[chunk(me_r), cols(me_p)]
         return remote(
             view, view, gw3_send.at[k], gw3_recv.at[lax.rem(me_r, owners)], row_dev(row_to(k))
         )
@@ -306,7 +322,7 @@
     guarded(me_r < owners, sum_rows)
 
     def total_chunk():
-        gw_blk[me_b] = gw_sum[...]
+        gw_blk[me_b] = gw_sum[:, cols(me_p)]
         for k in range(1, n_blk):
             src = blk_to(k)
             remote(
@@ -315,11 +331,24 @@
         total = gw_blk[0].astype(F32)
         for b in range(1, n_blk):
             total = total + gw_blk[b].astype(F32)
-        gw_all[chunk(me_r), :] = total.astype(BF)
+        gw_all[chunk(me_r), cols(me_p)] = total.astype(BF)
         for k in range(1, n_row):
             final_copy(k).start()
 
     guarded(me_r < owners, total_chunk)
+
+    for k in range(1, n_row):
+        src = row_to(k)
+
+        def wait_chunk(src=src, k=k):
+            view = gw_all.at[chunk(src), cols(me_p)]
+            remote(
+                view, view, gw3_send.at[k], gw3_recv.at[lax.rem(src, owners)], row_dev(src)
+            ).wait_recv()
+
+        guarded(src < owners, wait_chunk)
+    for k in range(1, n_rep):
+        core_copy(k).start()
 
     grad_feat = jnp.zeros((tile, wide), F32)
     for h in range(HALVES):
@@ -337,20 +366,16 @@
         )
     gf_ref[...] = grad_feat.astype(BF)
 
-    for k in range(1, n_row):
-        src = row_to(k)
-
-        def wait_chunk(src=src, k=k):
-            view = gw_all.at[chunk(src)]
-            remote(
-                view, view, gw3_send.at[k], gw3_recv.at[lax.rem(src, owners)], row_dev(src)
-            ).wait_recv()
-
-        guarded(src < owners, wait_chunk)
+    for k in range(1, n_rep):
+        p = lax.rem(me_p + k, n_rep)
+        view = gw_all.at[:, cols(p)]
+        remote(view, view, gw4_send.at[k], gw4_recv.at[p], blk_dev(blk_to(k))).wait_recv()
     gw_ref[...] = gw_all[...].astype(F32) * scale
 
     for c in sends:
         c.wait_send()
+    for k in range(1, n_rep):
+        core_copy(k).wait_send()
     for k in range(1, n_row):
         guarded(row_to(k) < owners, owner_copy(k).wait_send)
 
@@ -405,7 +430,7 @@
             pltpu.VMEM((wide, wide), BF),
             pltpu.VMEM((n_row, rows1, wide), BF),
             pltpu.VMEM((rows1, wide), BF),
-            pltpu.VMEM((n_blk, rows1, wide), BF),
+            pltpu.VMEM((n_blk, rows1, wide // n_rep), BF),
             pltpu.VMEM((wide, wide), BF),
             sem((4 + HALVES,)),
             sem((HALVES, n_row)),
@@ -422,6 +447,8 @@
             sem((n_blk,)),
             sem((n_row,)),
             sem((n_row,)),
+            sem((n_rep,)),
+            sem((n_rep,)),
         ],
         compiler_params=pltpu.CompilerParams(
             collective_id=0, has_side_effects=True, vmem_limit_bytes=60 * 1024 * 1024

time: 34.9 us -> 34.3 us (0.983)
  Pallas kernels: 31.4 us -> 30.8 us
    pallas_call x1, Pallas kernels: 31.4 us -> 30.8 us  [on_device(): pl.pallas_call(functools.partial(kernel, sizes), out_shape=(pltpu.VMEM((p...]
where the time goes in v3:
time: 34.3 us; the launch traced here: 34.1 us
  Pallas kernels  30.8 us (90%)
  local copies, waits for them, and re-layouts  1.96 us (6%)
  between operations  1.29 us (4%)
    pallas_call x1, Pallas kernels, on_device(): pl.pallas_call(functools.partial(kernel, sizes), out_shape=(pltpu.VMEM((p...  30.8 us
    unnamed x3, local copies, waits for them, and re-layouts  1.96 us

profile of v3, /device:TPU:0, one launch (start us, length us, event | category | flops | bytes accessed | tf_op | source)
XLA Modules:
  0.0 34.1 jit_solution(403137538446146594)
XLA Ops:
  1.3 30.8 %shard_map.103 = (bf16[128,256]{1,0:T(8,128)(2,1)S(1)}, bf16[128,256]{1,0:T(8,128)(2,1)S(1)}, f32[256,256]{1,0:T(8,128)S(1)}) custom-call(s32[16]{0:T(128)} %bitcast.8, s32[16]{0:T(128)} %bitcast.9, s32[1]{0:T(128)} %bitcast.5.count_ref, bf16[128,256]{1,0:T(8,128)(2,1)} %feat_hbm.1, bf16[128,256]{1,0:T(8,128)(2,1)} %cot_hbm.1, bf16[256,256]{1,0:T(8,128)(2,1)} %weight_hbm.1, ...), custom_call_target="tpu_custom_call" | custom-call | tf_op jit(solution)/shard_map/pallas_call | solution.py:407
  32.1 0.6 %copy.14 = bf16[128,256]{1,0:T(8,128)(2,1)} copy(bf16[128,256]{1,0:T(8,128)(2,1)S(1)} %get-tuple-element.3) | data formatting | bytes 131072
  32.7 0.6 %copy.15 = bf16[128,256]{1,0:T(8,128)(2,1)} copy(bf16[128,256]{1,0:T(8,128)(2,1)S(1)} %get-tuple-element.4) | data formatting | bytes 131072
  33.4 0.7 %copy.16 = f32[256,256]{1,0:T(8,128)} copy(f32[256,256]{1,0:T(8,128)S(1)} %get-tuple-element.5) | data formatting | bytes 524288
